TPU v7x, 32 devices: a whole 2x2x4 slice. The times are simulated.
32 devices in a mesh: dom: 8 (over z, x), blk: 4 (over y, core).
Axes of the slice: x: 2, y: 2, z: 4, core: 2. Of those that a mesh axis runs over, the one named last changes fastest.
Arguments:
- hessian: float32 [32, 15, 192, 192], P('dom')
- neighbours: int32 [32, 15], P('dom'), may hold values from 0 to 31, as said below
- counts: int32 [32], P('dom'), may hold values from 5 to 15
- basis_vectors: float32 [512, 6144], P('blk', 'dom')
Outputs:
- blocks: float32 [2, 64, 6144], P(None, 'blk', 'dom')
- factors: float32 [2, 64, 64], replicated
Inputs may be any that keep to these rules, and one draw needn't show every extreme that they name: `neighbours`: entry 0 of tile t's list is t itself; the others are distinct tiles of the domains within two of t's domain, cyclically, where tile t belongs to domain t // 4.
All inputs are finite; a program needn't handle non-finite values.
Results may differ from a plain program's by a relative error of at most 0.00024.
Values sent between devices are 32-bit elements; how exact they have to be, the bound alone decides.
A program may use at most 64 MiB of HBM per device.

v0:
```python
import jax
import jax.numpy as jnp
from jax import lax
from jax.sharding import PartitionSpec as P

BLOCK = 64
STORED = 512


finest = lax.Precision.HIGHEST


def passed_along(value, axis, by):
    peers = lax.axis_size(axis)
    return lax.ppermute(value, axis, [(i, (i + by) % peers) for i in range(peers)])


def neighbour_product(block_rows, hessian, neighbours, counts):
    dom_count = lax.axis_size("dom")
    me_dom = lax.axis_index("dom")
    tiles_own = hessian.shape[0]
    tile_rows = hessian.shape[2]
    col_count = block_rows.shape[0]
    pieces = []
    for offset in (2, 1, 0, -1, -2):
        if offset == 0:
            pieces.append(block_rows)
        else:
            pieces.append(passed_along(block_rows, "dom", offset))
    extended = jnp.concatenate(pieces, axis=1).reshape(col_count, 5 * tiles_own, tile_rows)
    owner_dom = neighbours // tiles_own
    slot_index = (owner_dom - me_dom + 2) % dom_count * tiles_own + neighbours % tiles_own
    chosen = jnp.take(extended, slot_index.reshape(-1), axis=1).reshape(
        col_count, tiles_own, neighbours.shape[1], tile_rows
    )
    live_mask = (jnp.arange(neighbours.shape[1])[None, :] < counts[:, None]).astype(jnp.float32)
    chosen = chosen * live_mask[None, :, :, None]
    result = jnp.einsum("tkij,btkj->bti", hessian, chosen, precision=finest)
    return result.reshape(col_count, tiles_own * tile_rows)


def local(hessian, neighbours, counts, basis_vectors):
    blk_count = lax.axis_size("blk")
    me_blk = lax.axis_index("blk")
    own_width = BLOCK // blk_count
    col_start = me_blk * own_width
    row_total = basis_vectors.shape[1] * lax.axis_size("dom")
    stored = lax.all_gather(basis_vectors, "blk", axis=0, tiled=True)
    current = lax.dynamic_slice_in_dim(stored, STORED - BLOCK + col_start, own_width, 0)
    blocks = []
    factors = []
    for lanczos_step in range(2):
        pending = neighbour_product(current, hessian, neighbours, counts)
        for sweep_index in range(2):
            partial_coef = jnp.dot(stored, pending.T, precision=finest)
            coefficients = lax.psum(partial_coef, "dom") / row_total
            pending = pending - jnp.dot(coefficients.T, stored, precision=finest)
        gathered = lax.all_gather(pending, "blk", axis=0, tiled=True)
        gram_block = lax.psum(jnp.dot(gathered, gathered.T, precision=finest), "dom") / row_total
        lower_factor = jnp.linalg.cholesky(gram_block)
        new_block = jax.scipy.linalg.solve_triangular(lower_factor, gathered, lower=True)
        current = lax.dynamic_slice_in_dim(new_block, col_start, own_width, 0)
        blocks.append(current)
        factors.append(lower_factor.T)
        stored = jnp.concatenate([new_block, stored[BLOCK:]], axis=0)
    return (jnp.stack(blocks), jnp.stack(factors))


def solution(mesh):
    placed = (P("dom", None, None, None), P("dom", None), P("dom"), P("blk", "dom"))
    return jax.shard_map(
        local, mesh=mesh, in_specs=placed, out_specs=(P(None, "blk", "dom"), P()), check_vma=False
    )
```

profile of v0, /device:TPU:0, one launch (start us, length us, event | category | flops | bytes accessed | tf_op | source)
XLA Modules:
  0.0 343.4 jit_solution(3650215497180829572)
XLA Ops:
  9.4 22.5 %all-gather.2.cloned.1.call-done = f32[512,768]{1,0:T(8,128)} async-done(((f32[128,768]{1,0:T(8,128)}), f32[512,768]{1,0:T(8,128)}) %all-gather.2.cloned.1.call-update) | async-done | bytes 1572880 | tf_op jit(solution)/shard_map/all_gather | solution.py:48
  32.9 1.5 collective-permute-start
  34.4 2.3 collective-permute-start.3
  36.7 2.4 collective-permute-start.2
  39.1 1.4 slice.16
  40.6 5.3 %collective-permute-done.1 = f32[16,768]{1,0:T(8,128)S(1)} collective-permute-done((f32[16,768]{1,0:T(8,128)S(1)}, f32[16,768]{1,0:T(8,128)S(1)}, u32[]{:S(2)}, u32[]{:S(2)}) %collective-permute-start.1) | collective-permute-done | bytes 49184 | tf_op jit(solution)/shard_map/ppermute | solution.py:15
  48.0 1.6 gather_fusion
  50.9 12.7 %convolution_bitcast_fusion.1 = f32[16,4,192]{2,0,1:T(8,128)S(1)} fusion(f32[4,15,192,192]{3,2,1,0:T(8,128)} %param.9, f32[16,4,15,192]{3,0,2,1:T(8,128)S(1)} %bitcast.67, f32[4,15]{1,0:T(4,128)S(1)} %fusion.29), kind=kOutput, calls=%fused_computation.4 | convolution fusion | flops 424857600 | bytes 9634032 | tf_op jit(solution)/shard_map/tkij,btkj->bti/dot_general | solution.py:38
  65.2 33.0 %psum.42 = f32[512,16]{0,1:T(8,128)S(1)} all-reduce(f32[512,16]{0,1:T(8,128)S(1)} %convolution_bitcast_fusion.3), channel_id=1, replica_groups=mesh['dom'=8,'blk'=4] {'dom'}, use_global_device_ids=true, to_apply=%region_0.2 | all-reduce | flops 8192 | bytes 65536 | tf_op jit(solution)/shard_map/psum | solution.py:56
  100.5 33.0 %psum.43 = f32[512,16]{0,1:T(8,128)S(1)} all-reduce(f32[512,16]{0,1:T(8,128)S(1)} %convolution_bitcast_fusion.2), channel_id=1, replica_groups=mesh['dom'=8,'blk'=4] {'dom'}, use_global_device_ids=true, to_apply=%region_1.3 | all-reduce | flops 8192 | bytes 65536 | tf_op jit(solution)/shard_map/psum | solution.py:56
  134.3 5.6 %all_gather.10 = f32[64,768]{1,0:T(8,128)S(1)} all-gather(f32[16,768]{1,0:T(8,128)S(1)} %convolution_subtract_fusion.2), channel_id=1, replica_groups=mesh['dom'=8,'blk'=4] {'blk'}, dimensions={0}, use_global_device_ids=true | all-gather | bytes 245760 | tf_op jit(solution)/shard_map/all_gather | solution.py:58
  140.3 33.2 %psum.44 = f32[64,64]{0,1:T(8,128)S(1)} all-reduce(f32[64,64]{0,1:T(8,128)S(1)} %fusion.38), channel_id=1, replica_groups=mesh['dom'=8,'blk'=4] {'dom'}, use_global_device_ids=true, to_apply=%region_2.4 | all-reduce | flops 4096 | bytes 32768 | tf_op jit(solution)/shard_map/psum | solution.py:59
  173.6 5.8 %cholesky.44 = f32[64,64]{1,0:T(8,128)S(1)} custom-call(f32[64,64]{1,0:T(8,128)S(1)} %fusion.11), custom_call_target="Cholesky" | custom-call | tf_op jit(solution)/shard_map/jit(cholesky)/cholesky | solution.py:60
  180.8 4.9 %custom-call.6 = f32[1,64,64]{1,2,0:T(8,128)S(1)} custom-call(f32[1,64,64]{2,1,0:T(8,128)S(1)} %get-tuple-element.10), custom_call_target="InvertDiagBlocksLowerTriangular" | custom-call | tf_op jit(solution)/shard_map/jit(_solve_triangular)/triangular_solve | solution.py:61
  186.2 2.3 collective-permute-start.6
  188.4 3.5 %collective-permute-start.7 = (f32[16,768]{1,0:T(8,128)S(1)}, f32[16,768]{1,0:T(8,128)S(1)}, u32[]{:S(2)}, u32[]{:S(2)}) collective-permute-start(f32[16,768]{1,0:T(8,128)S(1)} %constant_dynamic-slice_fusion), channel_id=1, source_target_pairs={{0,24},{4,28},{8,0},{12,4},{16,8},{20,12},{24,16},{28,20},{1,25},{... | collective-permute-start | bytes 147464 | tf_op jit(solution)/shard_map/ppermute | solution.py:15
  192.0 3.2 collective-permute-done.5
  196.3 12.7 %convolution_bitcast_fusion = f32[16,4,192]{2,0,1:T(8,128)S(1)} fusion(f32[4,15,192,192]{3,2,1,0:T(8,128)} %param.9, f32[16,4,15,192]{3,0,2,1:T(8,128)S(1)} %bitcast.66, f32[4,15]{1,0:T(4,128)S(1)} %fusion.29), kind=kOutput, calls=%fused_computation.3 | convolution fusion | flops 424857600 | bytes 9634032 | tf_op jit(solution)/shard_map/tkij,btkj->bti/dot_general | solution.py:38
  210.6 36.6 %psum.45 = f32[512,16]{0,1:T(8,128)S(1)} all-reduce(f32[512,16]{0,1:T(8,128)S(1)} %fusion.3), channel_id=1, replica_groups=mesh['dom'=8,'blk'=4] {'dom'}, use_global_device_ids=true, to_apply=%region_5.9 | all-reduce | flops 8192 | bytes 65536 | tf_op jit(solution)/shard_map/psum | solution.py:56
  249.5 33.2 %psum.46 = f32[512,16]{0,1:T(8,128)S(1)} all-reduce(f32[512,16]{0,1:T(8,128)S(1)} %fusion.2), channel_id=1, replica_groups=mesh['dom'=8,'blk'=4] {'dom'}, use_global_device_ids=true, to_apply=%region_6.10 | all-reduce | flops 8192 | bytes 65536 | tf_op jit(solution)/shard_map/psum | solution.py:56
  283.6 5.6 %all_gather.11 = f32[64,768]{1,0:T(8,128)S(1)} all-gather(f32[16,768]{1,0:T(8,128)S(1)} %convolution_subtract_fusion), channel_id=1, replica_groups=mesh['dom'=8,'blk'=4] {'blk'}, dimensions={0}, use_global_device_ids=true | all-gather | bytes 245760 | tf_op jit(solution)/shard_map/all_gather | solution.py:58
  289.5 33.0 %psum.47 = f32[64,64]{0,1:T(8,128)S(1)} all-reduce(f32[64,64]{0,1:T(8,128)S(1)} %fusion.39), channel_id=1, replica_groups=mesh['dom'=8,'blk'=4] {'dom'}, use_global_device_ids=true, to_apply=%region_7.11 | all-reduce | flops 4096 | bytes 32768 | tf_op jit(solution)/shard_map/psum | solution.py:59
  322.7 5.8 %cholesky.55 = f32[64,64]{1,0:T(8,128)S(1)} custom-call(f32[64,64]{1,0:T(8,128)S(1)} %fusion.8), custom_call_target="Cholesky" | custom-call | tf_op jit(solution)/shard_map/jit(cholesky)/cholesky | solution.py:60
  330.6 4.9 %custom-call.7 = f32[1,64,64]{1,2,0:T(8,128)S(1)} custom-call(f32[1,64,64]{2,1,0:T(8,128)S(1)} %get-tuple-element.12), custom_call_target="InvertDiagBlocksLowerTriangular" | custom-call | tf_op jit(solution)/shard_map/jit(_solve_triangular)/triangular_solve | solution.py:61
  (71 shorter events, 22.7 us)
Async XLA Ops:
  7.2 24.8 %all-gather.2.cloned.1.call-start = ((), (), s32[]{:S(2)}) async-start(), calls=%async_computation | async-start | bytes 1966080 | tf_op jit(solution)/shard_map/all_gather | solution.py:48
  32.0 14.0 %copy-start = (f32[512,768]{1,0:T(8,128)S(1)}, f32[512,768]{1,0:T(8,128)}, u32[]{:S(2)}) copy-start(f32[512,768]{1,0:T(8,128)} %all-gather.2.cloned.1.call-done) | copy-start | bytes 4718596
  32.9 7.7 %collective-permute-start = (f32[16,768]{1,0:T(8,128)S(1)}, f32[16,768]{1,0:T(8,128)S(1)}, u32[]{:S(2)}, u32[]{:S(2)}) collective-permute-start(f32[16,768]{1,0:T(8,128)S(1)} %constant_dynamic-slice_fusion.1), channel_id=1, source_target_pairs={{0,8},{4,12},{8,16},{12,20},{16,24},{20,28},{24,0},{28,4},{1,9},{5... | collective-permute-start | bytes 147464 | tf_op jit(solution)/shard_map/ppermute | solution.py:15
  34.4 11.6 %collective-permute-start.3 = (f32[16,768]{1,0:T(8,128)S(1)}, f32[16,768]{1,0:T(8,128)S(1)}, u32[]{:S(2)}, u32[]{:S(2)}) collective-permute-start(f32[16,768]{1,0:T(8,128)S(1)} %constant_dynamic-slice_fusion.1), channel_id=1, source_target_pairs={{0,24},{4,28},{8,0},{12,4},{16,8},{20,12},{24,16},{28,20},{1,25},{... | collective-permute-start | bytes 147464 | tf_op jit(solution)/shard_map/ppermute | solution.py:15
  36.7 9.3 %collective-permute-start.2 = (f32[16,768]{1,0:T(8,128)S(1)}, f32[16,768]{1,0:T(8,128)S(1)}, u32[]{:S(2)}, u32[]{:S(2)}) collective-permute-start(f32[16,768]{1,0:T(8,128)S(1)} %constant_dynamic-slice_fusion.1), channel_id=1, source_target_pairs={{0,28},{4,0},{8,4},{12,8},{16,12},{20,16},{24,20},{28,24},{1,29},{... | collective-permute-start | bytes 147464 | tf_op jit(solution)/shard_map/ppermute | solution.py:15
  39.1 6.8 %collective-permute-start.1 = (f32[16,768]{1,0:T(8,128)S(1)}, f32[16,768]{1,0:T(8,128)S(1)}, u32[]{:S(2)}, u32[]{:S(2)}) collective-permute-start(f32[16,768]{1,0:T(8,128)S(1)} %constant_dynamic-slice_fusion.1), channel_id=1, source_target_pairs={{0,4},{4,8},{8,12},{12,16},{16,20},{20,24},{24,28},{28,0},{1,5},{5... | collective-permute-start | bytes 147464 | tf_op jit(solution)/shard_map/ppermute | solution.py:15
  186.1 5.9 %collective-permute-start.4 = (f32[16,768]{1,0:T(8,128)S(1)}, f32[16,768]{1,0:T(8,128)S(1)}, u32[]{:S(2)}, u32[]{:S(2)}) collective-permute-start(f32[16,768]{1,0:T(8,128)S(1)} %constant_dynamic-slice_fusion), channel_id=1, source_target_pairs={{0,8},{4,12},{8,16},{12,20},{16,24},{20,28},{24,0},{28,4},{1,9},{5... | collective-permute-start | bytes 147464 | tf_op jit(solution)/shard_map/ppermute | solution.py:15
  186.2 9.1 %collective-permute-start.6 = (f32[16,768]{1,0:T(8,128)S(1)}, f32[16,768]{1,0:T(8,128)S(1)}, u32[]{:S(2)}, u32[]{:S(2)}) collective-permute-start(f32[16,768]{1,0:T(8,128)S(1)} %constant_dynamic-slice_fusion), channel_id=1, source_target_pairs={{0,28},{4,0},{8,4},{12,8},{16,12},{20,16},{24,20},{28,24},{1,29},{... | collective-permute-start | bytes 147464 | tf_op jit(solution)/shard_map/ppermute | solution.py:15
  188.4 6.8 %collective-permute-start.5 = (f32[16,768]{1,0:T(8,128)S(1)}, f32[16,768]{1,0:T(8,128)S(1)}, u32[]{:S(2)}, u32[]{:S(2)}) collective-permute-start(f32[16,768]{1,0:T(8,128)S(1)} %constant_dynamic-slice_fusion), channel_id=1, source_target_pairs={{0,4},{4,8},{8,12},{12,16},{16,20},{20,24},{24,28},{28,0},{1,5},{5... | collective-permute-start | bytes 147464 | tf_op jit(solution)/shard_map/ppermute | solution.py:15
  188.4 6.8 %collective-permute-start.7 = (f32[16,768]{1,0:T(8,128)S(1)}, f32[16,768]{1,0:T(8,128)S(1)}, u32[]{:S(2)}, u32[]{:S(2)}) collective-permute-start(f32[16,768]{1,0:T(8,128)S(1)} %constant_dynamic-slice_fusion), channel_id=1, source_target_pairs={{0,24},{4,28},{8,0},{12,4},{16,8},{20,12},{24,16},{28,20},{1,25},{... | collective-permute-start | bytes 147464 | tf_op jit(solution)/shard_map/ppermute | solution.py:15
Sparse Core Ops, SparseCore 0:
  9.6 22.3 all-gather.1
where the time goes:
time: 344 us; the launch traced here: 343 us
  blocking collectives  213 us (62%)
  matrix products  35.9 us (10%)
  waiting for transfers between devices  31.8 us (9%)
  other arithmetic  27.7 us (8%)
  between operations  14.3 us (4%)
  starting transfers between devices  12.2 us (4%)
  local copies, waits for them, and re-layouts  8.13 us (2%)
    psum x4, blocking collectives, local(): coefficients = lax.psum(partial_coef, 'dom') / row_total  136 us
    psum x2, blocking collectives, local(): lax.psum(jnp.dot(gathered, gathered.T, precision=finest), 'dom') / row_total  66.2 us
    dot_general x2, matrix products, neighbour_product(): result = jnp.einsum('tkij,btkj->bti', hessian, chosen, precision=finest)  25.4 us
    all_gather x1, waiting for transfers between devices, local(): stored = lax.all_gather(basis_vectors, 'blk', axis=0, tiled=True)  22.5 us
    another operation x6, other arithmetic, local(): lower_factor = jnp.linalg.cholesky(gram_block)  13 us
    ppermute x8, starting transfers between devices, passed_along(): lax.ppermute(value, axis, [(i, (i + by) % peers) for i in range(peers)])  12.1 us
    all_gather x2, blocking collectives, local(): gathered = lax.all_gather(pending, 'blk', axis=0, tiled=True)  11.2 us
    another operation x2, other arithmetic, local(): jax.scipy.linalg.solve_triangular(lower_factor, gathered, lower=True)  9.79 us
  transfers between devices with their start and end apart: 9, of which 3 were waited for; matrix products, arithmetic and copies ran while one was open for 1% of the time, Pallas kernels for 0%

commit v1 on v0

v1 whole, which is shorter than its diff:
```python
import functools

import jax
import jax.numpy as jnp
from jax import lax
from jax.experimental import pallas as pl
from jax.experimental.pallas import tpu as pltpu
from jax.sharding import PartitionSpec as P

BLOCK = 64
STORED = 512
STEPS = 2
SWEEPS = 2
PIECES = 8
SUB, LANE = 8, 128
f32, bf16 = jnp.float32, jnp.bfloat16
finest = lax.Precision.HIGHEST
NT = (((1,), (1,)), ((), ()))
NN = (((1,), (0,)), ((), ()))


def halves(value):
    high = value.astype(bf16)
    return high, (value - high.astype(f32)).astype(bf16)


def stacked(value):
    return jnp.concatenate(halves(value), axis=0)


def folded(double):
    rows = double.shape[0] // 2
    return double[:rows] + double[rows:]


def dot(left, right, dims):
    return lax.dot_general(left, right, dims, preferred_element_type=f32)


def factorize(gram):
    size = gram.shape[0]
    row_id = lax.broadcasted_iota(jnp.int32, (size, size), 0)
    col_id = lax.broadcasted_iota(jnp.int32, (size, size), 1)
    both = jnp.concatenate([gram, (row_id == col_id).astype(f32)], axis=1)
    groups = [both[SUB * g : SUB * g + SUB] for g in range(size // SUB)]
    sub_id = lax.broadcasted_iota(jnp.int32, (SUB, 2 * size), 0)
    for k in range(size):
        g, r = divmod(k, SUB)
        row = groups[g][r : r + 1]
        row = row * (1.0 / row[:, k : k + 1])
        if r < SUB - 1:
            column = groups[g][:, k : k + 1]
            groups[g] = jnp.where(sub_id > r, groups[g] - column * row, groups[g])
        for i in range(g + 1, len(groups)):
            groups[i] = groups[i] - groups[i][:, k : k + 1] * row
    both = jnp.concatenate(groups, axis=0)
    upper = both[:, :size]
    diagonal = jnp.sum(jnp.where(row_id == col_id, upper, 0.0), axis=1, keepdims=True)
    both = both * lax.rsqrt(diagonal)
    return jnp.where(col_id >= row_id, both[:, :size], 0.0), both[:, size:]


def kernel(
    dom_count, blk_count,
    slots_ref, hess_ref, basis_ref,
    blocks_ref, factors_ref,
    hess_f, hess_hi, hess_lo, share_in, ext, ext_b, prod, stored_f, stored_hi, stored_lo,
    part, rs_in, coef, pend, gram_in, new_full,
    hess_sem, x_s, x_r, st_s, st_r, halo_s, halo_r, rs_s, rs_r, ag_s, ag_r, pg_s, pg_r, gr_s, gr_r,
):
    tiles, listed, tile_rows, _ = hess_ref.shape
    per_blk, width = basis_ref.shape
    own = BLOCK // blk_count
    row_total = width * dom_count
    me_d, me_b = lax.axis_index("dom"), lax.axis_index("blk")
    sent = []

    def when(cond, do):
        if cond is None:
            do()
        else:
            pl.when(cond)(do)

    def remote(src, dst, send, recv, target):
        return pltpu.make_async_remote_copy(
            src_ref=src, dst_ref=dst, send_sem=send, recv_sem=recv,
            device_id=target, device_id_type=pl.DeviceIdType.MESH,
        )

    def send(cond, *what):
        copy = remote(*what)
        when(cond, copy.start)
        sent.append((cond, copy))

    for t in range(tiles):
        pltpu.make_async_copy(hess_ref.at[t], hess_f.at[t], hess_sem.at[t]).start()

    def dom_peer(o):
        return lax.rem(me_d + o + dom_count, dom_count)

    def blk_peer(o):
        return lax.rem(me_b + o + blk_count, blk_count)

    barrier = pltpu.get_barrier_semaphore()
    for o in range(1, dom_count):
        pl.semaphore_signal(barrier, inc=1, device_id=(dom_peer(o), me_b), device_id_type=pl.DeviceIdType.MESH)
    for o in range(1, blk_count):
        pl.semaphore_signal(barrier, inc=1, device_id=(me_d, blk_peer(o)), device_id_type=pl.DeviceIdType.MESH)
    pl.semaphore_wait(barrier, dom_count + blk_count - 2)

    last = blk_count - 1
    for j in range(last):
        rows = basis_ref.at[pl.ds(per_blk - BLOCK + own * j, own)]
        send(me_b == last, rows, share_in, x_s.at[j], x_r, (me_d, j))

    partner = me_b + 1 - 2 * lax.rem(me_b, 2)
    across = lax.rem(me_b + 2, 4)
    send(None, basis_ref, stored_f.at[me_b], st_s.at[0], st_r.at[0], (me_d, across))
    send(None, basis_ref, stored_f.at[me_b], st_s.at[1], st_r.at[1], (me_d, partner))
    stored_f[me_b] = basis_ref[...]

    @pl.when(me_b == last)
    def _():
        share_in[...] = basis_ref[per_blk - own :, :]

    @pl.when(me_b != last)
    def _():
        remote(share_in, share_in, x_s.at[0], x_r, (me_d, last)).wait_recv()

    def start_halo(step, share):
        for t in range(tiles):
            ext[step, 2, t] = share[:, t * tile_rows : (t + 1) * tile_rows]
        for i, o in enumerate((2, -2, 1, -1)):
            send(None, ext.at[step, 2], ext.at[step, 2 - o], halo_s.at[step, i], halo_r.at[step, i], (dom_peer(o), me_b))

    def split_ext(step, i):
        for t in range(tiles):
            ext_b[i * tiles + t] = stacked(ext[step, i, t])

    def end_halo(step):
        split_ext(step, 2)
        for i, o in enumerate((2, -2, 1, -1)):
            remote(ext.at[step, 2], ext.at[step, 2 - o], halo_s.at[step, i], halo_r.at[step, i], (dom_peer(-o), me_b)).wait_recv()
            split_ext(step, 2 - o)

    def product():
        @pl.loop(0, tiles)
        def _(t):
            total = jnp.zeros((2 * own, tile_rows), f32)
            for k in range(listed):
                x = ext_b[slots_ref[t * listed + k]]
                total += dot(x, hess_hi[t, k], NT) + dot(x, hess_lo[t, k], NT)
            prod[t] = folded(total)

        return jnp.concatenate([prod[t] for t in range(tiles)], axis=1)

    def summed(a, value):
        lanes = STORED // LANE
        for j in range(PIECES):
            h, q = divmod(j, lanes)
            part[a, j] = value[h * SUB : (h + 1) * SUB, q * LANE : (q + 1) * LANE]
        all_own = dom_count <= PIECES
        for o in range(1, dom_count):
            to = dom_peer(o)
            cond = None if all_own else to < PIECES
            piece = to if all_own else lax.rem(to, PIECES)
            send(cond, part.at[a, piece], rs_in.at[a, o], rs_s.at[a, o], rs_r.at[a, o], (to, me_b))
        mine = me_d if all_own else lax.rem(me_d, PIECES)
        owner = None if all_own else me_d < PIECES

        def reduce():
            total = part[a, mine]
            for o in range(1, dom_count):
                remote(part.at[a, 0], rs_in.at[a, o], rs_s.at[a, o], rs_r.at[a, o], (dom_peer(-o), me_b)).wait_recv()
                total += rs_in[a, o]
            coef[a, mine] = total / row_total

        when(owner, reduce)
        for o in range(1, dom_count):
            send(owner, coef.at[a, mine], coef.at[a, mine], ag_s.at[a, o], ag_r.at[a, o], (dom_peer(o), me_b))
        for o in range(1, dom_count):
            origin = dom_peer(-o)
            cond = None if all_own else origin < PIECES
            copy = remote(coef.at[a, 0], coef.at[a, 0], ag_s.at[a, o], ag_r.at[a, o], (origin, me_b))
            when(cond, copy.wait_recv)
        return jnp.concatenate(
            [jnp.concatenate([coef[a, h * lanes + q] for q in range(lanes)], axis=1) for h in range(PIECES // lanes)], axis=0
        )

    start_halo(0, share_in[...])
    ext_b[5 * tiles] = jnp.zeros(ext_b.shape[1:], bf16)
    for t in range(tiles):
        pltpu.make_async_copy(hess_ref.at[t], hess_f.at[t], hess_sem.at[t]).wait()

        @pl.loop(0, listed)
        def _(k):
            high, low = halves(hess_f[t, k])
            hess_hi[t, k] = high
            hess_lo[t, k] = low

    for step in range(STEPS):
        end_halo(step)
        pending = product()
        if step == 0:
            remote(basis_ref, stored_f.at[0], st_s.at[0], st_r.at[0], (me_d, across)).wait_recv()
            send(None, stored_f.at[across], stored_f.at[across], st_s.at[2], st_r.at[2], (me_d, partner))
            for i in (1, 2):
                remote(basis_ref, stored_f.at[0], st_s.at[i], st_r.at[i], (me_d, partner)).wait_recv()
            for i in range(blk_count):
                high, low = halves(stored_f[i])
                stored_hi[i * per_blk : (i + 1) * per_blk] = high
                stored_lo[i * per_blk : (i + 1) * per_blk] = low
        for sweep in range(SWEEPS):
            both = stacked(pending)
            inner = folded(dot(both, stored_hi[...], NT) + dot(both, stored_lo[...], NT))
            both = stacked(summed(SWEEPS * step + sweep, inner))
            pending = pending - folded(dot(both, stored_hi[...], NN) + dot(both, stored_lo[...], NN))
        pend[step, me_b] = pending
        for o in range(1, blk_count):
            send(None, pend.at[step, me_b], pend.at[step, me_b], pg_s.at[step, o], pg_r.at[step, o], (me_d, blk_peer(o)))
        for o in range(1, blk_count):
            remote(pend.at[step, 0], pend.at[step, 0], pg_s.at[step, o], pg_r.at[step, o], (me_d, blk_peer(-o))).wait_recv()
        full = jnp.concatenate([pend[step, i] for i in range(blk_count)], axis=0)
        high, low = halves(full)
        cross = dot(high, low, NT)
        gram_part = dot(high, high, NT) + cross + cross.T
        half = BLOCK // 2
        gram_in[step, me_d] = jnp.concatenate([gram_part[:half], gram_part[half:]], axis=1)
        for o in range(1, dom_count):
            send(None, gram_in.at[step, me_d], gram_in.at[step, me_d], gr_s.at[step, o], gr_r.at[step, o], (dom_peer(o), me_b))
        for o in range(1, dom_count):
            remote(gram_in.at[step, 0], gram_in.at[step, 0], gr_s.at[step, o], gr_r.at[step, o], (dom_peer(-o), me_b)).wait_recv()
        total = gram_in[step, 0]
        for d in range(1, dom_count):
            total += gram_in[step, d]
        total = total / row_total
        gram = jnp.concatenate([total[:, :BLOCK], total[:, BLOCK:]], axis=0)
        upper, inverse = factorize(gram)
        factors_ref[step] = upper
        new = lax.dot_general(inverse, full, NN, precision=finest, preferred_element_type=f32)
        new_full[step] = new
        share = new_full[step, pl.ds(pl.multiple_of(me_b * own, own), own), :]
        blocks_ref[step] = share
        if step + 1 < STEPS:
            start_halo(step + 1, share)
            high, low = halves(new)
            stored_hi[:BLOCK] = high
            stored_lo[:BLOCK] = low

    for cond, copy in sent:
        when(cond, copy.wait_send)


def local(hessian, neighbours, counts, basis_vectors):
    dom_count = lax.axis_size("dom")
    blk_count = lax.axis_size("blk")
    me_dom = lax.axis_index("dom")
    tiles, listed, tile_rows, _ = hessian.shape
    per_blk, width = basis_vectors.shape
    own = BLOCK // blk_count
    slot = (neighbours // tiles - me_dom + 2) % dom_count * tiles + neighbours % tiles
    live = jnp.arange(listed)[None, :] < counts[:, None]
    slots = jnp.where(live, slot, 5 * tiles).reshape(-1).astype(jnp.int32)
    sums = STEPS * SWEEPS
    dma = pltpu.SemaphoreType.DMA
    vmem = pl.BlockSpec(memory_space=pltpu.VMEM)
    return pl.pallas_call(
        functools.partial(kernel, dom_count, blk_count),
        out_shape=(
            jax.ShapeDtypeStruct((STEPS, own, width), f32),
            jax.ShapeDtypeStruct((STEPS, BLOCK, BLOCK), f32),
        ),
        in_specs=[pl.BlockSpec(memory_space=pltpu.SMEM), pl.BlockSpec(memory_space=pl.ANY), vmem],
        out_specs=(vmem, vmem),
        scratch_shapes=[
            pltpu.VMEM(hessian.shape, f32),
            pltpu.VMEM(hessian.shape, bf16),
            pltpu.VMEM(hessian.shape, bf16),
            pltpu.VMEM((own, width), f32),
            pltpu.VMEM((STEPS, 5, tiles, own, tile_rows), f32),
            pltpu.VMEM((5 * tiles + 1, 2 * own, tile_rows), bf16),
            pltpu.VMEM((tiles, own, tile_rows), f32),
            pltpu.VMEM((blk_count, per_blk, width), f32),
            pltpu.VMEM((STORED, width), bf16),
            pltpu.VMEM((STORED, width), bf16),
            pltpu.VMEM((sums, PIECES, SUB, LANE), f32),
            pltpu.VMEM((sums, dom_count, SUB, LANE), f32),
            pltpu.VMEM((sums, PIECES, SUB, LANE), f32),
            pltpu.VMEM((STEPS, blk_count, own, width), f32),
            pltpu.VMEM((STEPS, dom_count, BLOCK // 2, 2 * BLOCK), f32),
            pltpu.VMEM((STEPS, BLOCK, width), f32),
            dma((tiles,)),
            dma((blk_count,)), dma,
            dma((3,)), dma((3,)),
            dma((STEPS, 4)), dma((STEPS, 4)),
            dma((sums, dom_count)), dma((sums, dom_count)),
            dma((sums, dom_count)), dma((sums, dom_count)),
            dma((STEPS, blk_count)), dma((STEPS, blk_count)),
            dma((STEPS, dom_count)), dma((STEPS, dom_count)),
        ],
        compiler_params=pltpu.CompilerParams(
            collective_id=0, has_side_effects=True, vmem_limit_bytes=56 * 1024 * 1024
        ),
        name="lanczos",
    )(slots, hessian, basis_vectors)


def solution(mesh):
    placed = (P("dom", None, None, None), P("dom", None), P("dom"), P("blk", "dom"))
    return jax.shard_map(
        local, mesh=mesh, in_specs=placed, out_specs=(P(None, "blk", "dom"), P()), check_vma=False
    )
```

time: 344 us -> 105 us (0.31)
  blocking collectives: 213 us -> 0 us
  Pallas kernels: 0 us -> 99.6 us
  matrix products: 35.9 us -> 0 us
  waiting for transfers between devices: 31.8 us -> 0 us
  other arithmetic: 27.7 us -> 0.76 us
  between operations: 14.3 us -> 0.64 us
  starting transfers between devices: 12.2 us -> 0 us
  local copies, waits for them, and re-layouts: 8.13 us -> 3.61 us
    psum x6 -> x0, blocking collectives: 202 us -> none  [the longest x4 136 us: local(): coefficients = lax.psum(partial_coef, 'dom') / row_total]
    pallas_call x0 -> x1, Pallas kernels: none -> 99.6 us  [local(): pl.pallas_call(functools.partial(kernel, dom_count, blk_count), out_shape...]
    dot_general x12 -> x0, matrix products: 35.1 us -> none  [the longest x2 25.4 us: neighbour_product(): result = jnp.einsum('tkij,btkj->bti', hessian, chosen, precision=finest)]
    another operation x12 -> x0, other arithmetic: 24.8 us -> none  [the longest x6 13 us: local(): lower_factor = jnp.linalg.cholesky(gram_block)]
    all_gather x1 -> x0, waiting for transfers between devices: 22.5 us -> none  [local(): stored = lax.all_gather(basis_vectors, 'blk', axis=0, tiled=True)]
    ppermute x8 -> x0, starting transfers between devices: 12.1 us -> none  [passed_along(): lax.ppermute(value, axis, [(i, (i + by) % peers) for i in range(peers)])]
    all_gather x2 -> x0, blocking collectives: 11.2 us -> none  [local(): gathered = lax.all_gather(pending, 'blk', axis=0, tiled=True)]
    ppermute x8 -> x0, waiting for transfers between devices: 8.59 us -> none  [passed_along(): lax.ppermute(value, axis, [(i, (i + by) % peers) for i in range(peers)])]
  transfers between devices with their start and end apart: 9 -> 0, of which waited for: 3 -> 0; matrix products, arithmetic and copies ran while one was open for 1% -> 0% of each run, Pallas kernels for 0% -> 0%
where the time goes in v1:
time: 105 us
  Pallas kernels  99.6 us (95%)
  local copies, waits for them, and re-layouts  3.61 us (3%)
    pallas_call x1, Pallas kernels, local(): pl.pallas_call(functools.partial(kernel, dom_count, blk_count), out_shape...  99.6 us
    unnamed x2, local copies, waits for them, and re-layouts  3.01 us

profile of v1, /device:TPU:0, one launch (start us, length us, event | category | flops | bytes accessed | tf_op | source)
XLA Modules:
  0.0 104.6 jit_solution(10727923639878110322)
XLA Ops:
  0.6 0.8 fusion.5
  1.4 0.6 reshape.8.slots_ref
  2.0 99.6 %lanczos.1 = (f32[2,16,768]{2,1,0:T(8,128)}, f32[2,64,64]{2,1,0:T(8,128)}) custom-call(s32[60]{0:T(128)} %reshape.8.slots_ref, f32[4,15,192,192]{3,2,1,0:T(8,128)} %hess_ref.1, f32[128,768]{1,0:T(8,128)} %basis_ref.1), custom_call_target="tpu_custom_call" | custom-call | tf_op jit(solution)/shard_map/lanczos/pallas_call | solution.py:267
  101.6 1.5 %copy.8 = f32[2,16,768]{2,1,0:T(8,128)} copy(f32[2,16,768]{2,1,0:T(8,128)} %get-tuple-element.4) | data formatting | bytes 196608
  103.1 1.5 %copy.9 = f32[2,64,64]{2,1,0:T(8,128)} copy(f32[2,64,64]{2,1,0:T(8,128)} %get-tuple-element.5) | data formatting | bytes 65536

commit v2 on v1

--- a/solution.py
+++ b/solution.py
@@ -44,15 +44,24 @@
     both = jnp.concatenate([gram, (row_id == col_id).astype(f32)], axis=1)
     groups = [both[SUB * g : SUB * g + SUB] for g in range(size // SUB)]
     sub_id = lax.broadcasted_iota(jnp.int32, (SUB, 2 * size), 0)
-    for k in range(size):
+    spread = (SUB, 2 * size)
+    for k in range(0, size, 2):
         g, r = divmod(k, SUB)
-        row = groups[g][r : r + 1]
-        row = row * (1.0 / row[:, k : k + 1])
-        if r < SUB - 1:
-            column = groups[g][:, k : k + 1]
-            groups[g] = jnp.where(sub_id > r, groups[g] - column * row, groups[g])
-        for i in range(g + 1, len(groups)):
-            groups[i] = groups[i] - groups[i][:, k : k + 1] * row
+        first = {i: jnp.broadcast_to(groups[i][:, k : k + 1], spread) for i in range(g, len(groups))}
+        second = {i: jnp.broadcast_to(groups[i][:, k + 1 : k + 2], spread) for i in range(g, len(groups))}
+        row0, row1 = groups[g][r : r + 1], groups[g][r + 1 : r + 2]
+        inverse0 = 1.0 / first[g][r : r + 1]
+        below = first[g][r + 1 : r + 2]
+        scale = below * inverse0
+        inverse1 = 1.0 / (second[g][r + 1 : r + 2] - scale * below)
+        row1 = row1 - scale * row0
+        solved1 = row1 * inverse1
+        solved0 = row0 * inverse0 - scale * solved1
+        for i in range(g, len(groups)):
+            rest = groups[i] - first[i] * solved0 - second[i] * solved1
+            if i == g:
+                rest = jnp.where(sub_id > r + 1, rest, jnp.where(sub_id == r + 1, row1, groups[i]))
+            groups[i] = rest
     both = jnp.concatenate(groups, axis=0)
     upper = both[:, :size]
     diagonal = jnp.sum(jnp.where(row_id == col_id, upper, 0.0), axis=1, keepdims=True)
@@ -143,16 +152,20 @@
             remote(ext.at[step, 2], ext.at[step, 2 - o], halo_s.at[step, i], halo_r.at[step, i], (dom_peer(-o), me_b)).wait_recv()
             split_ext(step, 2 - o)
 
-    def product():
-        @pl.loop(0, tiles)
+    def product(first, end):
+        @pl.loop(first, end)
         def _(t):
-            total = jnp.zeros((2 * own, tile_rows), f32)
+            total = jnp.zeros((tile_rows, 2 * own), f32)
             for k in range(listed):
                 x = ext_b[slots_ref[t * listed + k]]
-                total += dot(x, hess_hi[t, k], NT) + dot(x, hess_lo[t, k], NT)
-            prod[t] = folded(total)
-
-        return jnp.concatenate([prod[t] for t in range(tiles)], axis=1)
+                total += dot(hess_hi[t, k], x, NT) + dot(hess_lo[t, k], x, NT)
+            prod[t] = folded(total.T)
+
+    def split_stored(i):
+        high, low = halves(stored_f[i])
+        rows = pl.ds(pl.multiple_of(i * per_blk, per_blk), per_blk)
+        stored_hi[rows] = high
+        stored_lo[rows] = low
 
     def summed(a, value):
         lanes = STORED // LANE
@@ -198,21 +211,23 @@
             hess_hi[t, k] = high
             hess_lo[t, k] = low
 
+    split_stored(me_b)
     for step in range(STEPS):
         end_halo(step)
-        pending = product()
+        product(0, tiles // 2)
         if step == 0:
             remote(basis_ref, stored_f.at[0], st_s.at[0], st_r.at[0], (me_d, across)).wait_recv()
             send(None, stored_f.at[across], stored_f.at[across], st_s.at[2], st_r.at[2], (me_d, partner))
-            for i in (1, 2):
+        product(tiles // 2, tiles)
+        pending = jnp.concatenate([prod[t] for t in range(tiles)], axis=1)
+        if step == 0:
+            split_stored(across)
+            for i, origin in ((1, partner), (2, lax.rem(partner + 2, 4))):
                 remote(basis_ref, stored_f.at[0], st_s.at[i], st_r.at[i], (me_d, partner)).wait_recv()
-            for i in range(blk_count):
-                high, low = halves(stored_f[i])
-                stored_hi[i * per_blk : (i + 1) * per_blk] = high
-                stored_lo[i * per_blk : (i + 1) * per_blk] = low
+                split_stored(origin)
         for sweep in range(SWEEPS):
             both = stacked(pending)
-            inner = folded(dot(both, stored_hi[...], NT) + dot(both, stored_lo[...], NT))
+            inner = folded((dot(stored_hi[...], both, NT) + dot(stored_lo[...], both, NT)).T)
             both = stacked(summed(SWEEPS * step + sweep, inner))
             pending = pending - folded(dot(both, stored_hi[...], NN) + dot(both, stored_lo[...], NN))
         pend[step, me_b] = pending

time: 105 us -> 102 us (0.971)
  Pallas kernels: 99.6 us -> 96.6 us
    pallas_call x1, Pallas kernels: 99.6 us -> 96.6 us  [local(): pl.pallas_call(functools.partial(kernel, dom_count, blk_count), out_shape...]
where the time goes in v2:
time: 102 us
  Pallas kernels  96.6 us (95%)
  local copies, waits for them, and re-layouts  3.61 us (4%)
    pallas_call x1, Pallas kernels, local(): pl.pallas_call(functools.partial(kernel, dom_count, blk_count), out_shape...  96.6 us
    unnamed x2, local copies, waits for them, and re-layouts  3.01 us

profile of v2, /device:TPU:0, one launch (start us, length us, event | category | flops | bytes accessed | tf_op | source)
XLA Modules:
  0.0 101.6 jit_solution(8999709455802075996)
XLA Ops:
  0.6 0.8 fusion.5
  1.4 0.6 reshape.8.slots_ref
  2.0 96.6 %lanczos.1 = (f32[2,16,768]{2,1,0:T(8,128)}, f32[2,64,64]{2,1,0:T(8,128)}) custom-call(s32[60]{0:T(128)} %reshape.8.slots_ref, f32[4,15,192,192]{3,2,1,0:T(8,128)} %hess_ref.1, f32[128,768]{1,0:T(8,128)} %basis_ref.1), custom_call_target="tpu_custom_call" | custom-call | tf_op jit(solution)/shard_map/lanczos/pallas_call | solution.py:282
  98.6 1.5 %copy.8 = f32[2,16,768]{2,1,0:T(8,128)} copy(f32[2,16,768]{2,1,0:T(8,128)} %get-tuple-element.4) | data formatting | bytes 196608
  100.1 1.5 %copy.9 = f32[2,64,64]{2,1,0:T(8,128)} copy(f32[2,64,64]{2,1,0:T(8,128)} %get-tuple-element.5) | data formatting | bytes 65536

commit v3 on v2

--- a/solution.py
+++ b/solution.py
@@ -74,8 +74,9 @@
     slots_ref, hess_ref, basis_ref,
     blocks_ref, factors_ref,
     hess_f, hess_hi, hess_lo, share_in, ext, ext_b, prod, stored_f, stored_hi, stored_lo,
-    part, rs_in, coef, pend, gram_in, new_full,
+    part, rs_in, coef, pend, gram_in, new_full, own_coef, mat_part, mat_in, mat_all, mat, mat_hi, mat_lo,
     hess_sem, x_s, x_r, st_s, st_r, halo_s, halo_r, rs_s, rs_r, ag_s, ag_r, pg_s, pg_r, gr_s, gr_r,
+    cg_s, cg_r, ms_s, ms_r, mg_s, mg_r, mb_s, mb_r,
 ):
     tiles, listed, tile_rows, _ = hess_ref.shape
     per_blk, width = basis_ref.shape
@@ -167,19 +168,123 @@
         stored_hi[rows] = high
         stored_lo[rows] = low
 
-    def summed(a, value):
+    all_own = dom_count <= PIECES
+    mine = me_d if all_own else lax.rem(me_d, PIECES)
+    owner = None if all_own else me_d < PIECES
+
+    def scatter_mat():
+        rows = pl.ds(pl.multiple_of(me_b * per_blk, per_blk), per_blk)
+        high, low = stored_hi[rows], stored_lo[rows]
+        value = dot(high, stored_hi[...], NT) + dot(high, stored_lo[...], NT) + dot(low, stored_hi[...], NT)
+        each = per_blk // PIECES
+        for j in range(PIECES):
+            mat_part[j] = value[j * each : (j + 1) * each]
+        for o in range(1, dom_count):
+            to = dom_peer(o)
+            cond = None if all_own else to < PIECES
+            piece = to if all_own else lax.rem(to, PIECES)
+            send(cond, mat_part.at[piece], mat_in.at[o], ms_s.at[o], ms_r.at[o], (to, me_b))
+
+    def reduce_mat():
+        def reduce():
+            total = mat_part[mine]
+            for o in range(1, dom_count):
+                remote(mat_part.at[0], mat_in.at[o], ms_s.at[o], ms_r.at[o], (dom_peer(-o), me_b)).wait_recv()
+                total += mat_in[o]
+            mat_all[me_b, mine] = total / row_total
+
+        when(owner, reduce)
+        for o in range(1, dom_count):
+            piece = mat_all.at[me_b, mine]
+            send(owner, piece, piece, mg_s.at[o], mg_r.at[o], (dom_peer(o), me_b))
+
+    def spread_mat():
+        for o in range(1, dom_count):
+            origin = dom_peer(-o)
+            cond = None if all_own else origin < PIECES
+            piece = mat_all.at[me_b, 0]
+            when(cond, remote(piece, piece, mg_s.at[o], mg_r.at[o], (origin, me_b)).wait_recv)
+        for o in range(1, blk_count):
+            send(None, mat_all.at[me_b], mat_all.at[me_b], mb_s.at[o], mb_r.at[o], (me_d, blk_peer(o)))
+
+    def times_mat(value):
+        both = stacked(value)
+        return folded(dot(both, mat_hi[...], NN) + dot(both, mat_lo[...], NN))
+
+    def split_mat():
+        high, low = halves(mat[...])
+        mat_hi[...] = high
+        mat_lo[...] = low
+
+    def replace_mat(inverse):
+        for o in range(1, blk_count):
+            remote(mat_all.at[0], mat_all.at[0], mb_s.at[o], mb_r.at[o], (me_d, blk_peer(-o))).wait_recv()
+        each = per_blk // PIECES
+        for i in range(blk_count):
+            for j in range(PIECES):
+                mat[i * per_blk + j * each : i * per_blk + (j + 1) * each] = mat_all[i, j]
+        split_mat()
+        second = all_coef(0)
+        rows = lax.dot_general(
+            inverse, second - times_mat(second), NN, precision=finest, preferred_element_type=f32
+        )
+        mat[:, : 2 * BLOCK] = jnp.concatenate([rows.T, mat[:, BLOCK : 2 * BLOCK]], axis=1)
+        unit = lax.broadcasted_iota(jnp.int32, (BLOCK, BLOCK), 0) == lax.broadcasted_iota(jnp.int32, (BLOCK, BLOCK), 1)
+        mat[:BLOCK] = jnp.concatenate([unit.astype(f32), rows[:, BLOCK:]], axis=1)
+        split_mat()
+
+    def send_coef(step, value):
+        own_coef[step, me_b] = value
+        for o in range(1, blk_count):
+            piece = own_coef.at[step, me_b]
+            send(None, piece, piece, cg_s.at[step, o], cg_r.at[step, o], (me_d, blk_peer(o)))
+
+    def all_coef(step):
+        for o in range(1, blk_count):
+            piece = own_coef.at[step, 0]
+            remote(piece, piece, cg_s.at[step, o], cg_r.at[step, o], (me_d, blk_peer(-o))).wait_recv()
+        return jnp.concatenate([own_coef[step, i] for i in range(blk_count)], axis=0)
+
+    def send_pending(step, pending):
+        pend[step, me_b] = pending
+        for o in range(1, blk_count):
+            piece = pend.at[step, me_b]
+            send(None, piece, piece, pg_s.at[step, o], pg_r.at[step, o], (me_d, blk_peer(o)))
+
+    def send_gram(step):
+        for o in range(1, blk_count):
+            remote(pend.at[step, 0], pend.at[step, 0], pg_s.at[step, o], pg_r.at[step, o], (me_d, blk_peer(-o))).wait_recv()
+        full = jnp.concatenate([pend[step, i] for i in range(blk_count)], axis=0)
+        high, low = halves(full)
+        cross = dot(high, low, NT)
+        gram_part = dot(high, high, NT) + cross + cross.T
+        half = BLOCK // 2
+        gram_in[step, me_d] = jnp.concatenate([gram_part[:half], gram_part[half:]], axis=1)
+        for o in range(1, dom_count):
+            piece = gram_in.at[step, me_d]
+            send(None, piece, piece, gr_s.at[step, o], gr_r.at[step, o], (dom_peer(o), me_b))
+
+    def end_gram(step):
+        for o in range(1, dom_count):
+            piece = gram_in.at[step, 0]
+            remote(piece, piece, gr_s.at[step, o], gr_r.at[step, o], (dom_peer(-o), me_b)).wait_recv()
+        total = gram_in[step, 0]
+        for d in range(1, dom_count):
+            total += gram_in[step, d]
+        total = total / row_total
+        return jnp.concatenate([total[:, :BLOCK], total[:, BLOCK:]], axis=0)
+
+    def summed(a, value, meanwhile):
         lanes = STORED // LANE
         for j in range(PIECES):
             h, q = divmod(j, lanes)
             part[a, j] = value[h * SUB : (h + 1) * SUB, q * LANE : (q + 1) * LANE]
-        all_own = dom_count <= PIECES
         for o in range(1, dom_count):
             to = dom_peer(o)
             cond = None if all_own else to < PIECES
             piece = to if all_own else lax.rem(to, PIECES)
             send(cond, part.at[a, piece], rs_in.at[a, o], rs_s.at[a, o], rs_r.at[a, o], (to, me_b))
-        mine = me_d if all_own else lax.rem(me_d, PIECES)
-        owner = None if all_own else me_d < PIECES
+        meanwhile()
 
         def reduce():
             total = part[a, mine]
@@ -225,31 +330,34 @@
             for i, origin in ((1, partner), (2, lax.rem(partner + 2, 4))):
                 remote(basis_ref, stored_f.at[0], st_s.at[i], st_r.at[i], (me_d, partner)).wait_recv()
                 split_stored(origin)
-        for sweep in range(SWEEPS):
+        if step == 0:
+            for sweep, meanwhile in enumerate((scatter_mat, reduce_mat)):
+                both = stacked(pending)
+                inner = folded((dot(stored_hi[...], both, NT) + dot(stored_lo[...], both, NT)).T)
+                coefficients = summed(sweep, inner, meanwhile)
+                both = stacked(coefficients)
+                pending = pending - folded(dot(both, stored_hi[...], NN) + dot(both, stored_lo[...], NN))
+            send_pending(step, pending)
+            send_coef(step, coefficients)
+            send_gram(step)
+            spread_mat()
+            gram = end_gram(step)
+            full = jnp.concatenate([pend[step, i] for i in range(blk_count)], axis=0)
+        else:
+            send_pending(step, pending)
             both = stacked(pending)
             inner = folded((dot(stored_hi[...], both, NT) + dot(stored_lo[...], both, NT)).T)
-            both = stacked(summed(SWEEPS * step + sweep, inner))
-            pending = pending - folded(dot(both, stored_hi[...], NN) + dot(both, stored_lo[...], NN))
-        pend[step, me_b] = pending
-        for o in range(1, blk_count):
-            send(None, pend.at[step, me_b], pend.at[step, me_b], pg_s.at[step, o], pg_r.at[step, o], (me_d, blk_peer(o)))
-        for o in range(1, blk_count):
-            remote(pend.at[step, 0], pend.at[step, 0], pg_s.at[step, o], pg_r.at[step, o], (me_d, blk_peer(-o))).wait_recv()
-        full = jnp.concatenate([pend[step, i] for i in range(blk_count)], axis=0)
-        high, low = halves(full)
-        cross = dot(high, low, NT)
-        gram_part = dot(high, high, NT) + cross + cross.T
-        half = BLOCK // 2
-        gram_in[step, me_d] = jnp.concatenate([gram_part[:half], gram_part[half:]], axis=1)
-        for o in range(1, dom_count):
-            send(None, gram_in.at[step, me_d], gram_in.at[step, me_d], gr_s.at[step, o], gr_r.at[step, o], (dom_peer(o), me_b))
-        for o in range(1, dom_count):
-            remote(gram_in.at[step, 0], gram_in.at[step, 0], gr_s.at[step, o], gr_r.at[step, o], (dom_peer(-o), me_b)).wait_recv()
-        total = gram_in[step, 0]
-        for d in range(1, dom_count):
-            total += gram_in[step, d]
-        total = total / row_total
-        gram = jnp.concatenate([total[:, :BLOCK], total[:, BLOCK:]], axis=0)
+            send_coef(step, summed(SWEEPS, inner, functools.partial(send_gram, step)))
+            first = all_coef(step)
+            second = first - times_mat(first)
+            left = second - times_mat(second)
+            coefficients = first + second
+            both = stacked(coefficients)
+            full = jnp.concatenate([pend[step, i] for i in range(blk_count)], axis=0)
+            full = full - folded(dot(both, stored_hi[...], NN) + dot(both, stored_lo[...], NN))
+            gram = end_gram(step)
+            gram -= lax.dot_general(coefficients, first, NT, precision=finest, preferred_element_type=f32)
+            gram -= lax.dot_general(left, coefficients, NT, precision=finest, preferred_element_type=f32)
         upper, inverse = factorize(gram)
         factors_ref[step] = upper
         new = lax.dot_general(inverse, full, NN, precision=finest, preferred_element_type=f32)
@@ -261,6 +369,7 @@
             high, low = halves(new)
             stored_hi[:BLOCK] = high
             stored_lo[:BLOCK] = low
+            replace_mat(inverse)
 
     for cond, copy in sent:
         when(cond, copy.wait_send)
@@ -276,7 +385,8 @@
     slot = (neighbours // tiles - me_dom + 2) % dom_count * tiles + neighbours % tiles
     live = jnp.arange(listed)[None, :] < counts[:, None]
     slots = jnp.where(live, slot, 5 * tiles).reshape(-1).astype(jnp.int32)
-    sums = STEPS * SWEEPS
+    sums = STEPS * SWEEPS - 1
+    each = per_blk // PIECES
     dma = pltpu.SemaphoreType.DMA
     vmem = pl.BlockSpec(memory_space=pltpu.VMEM)
     return pl.pallas_call(
@@ -304,6 +414,13 @@
             pltpu.VMEM((STEPS, blk_count, own, width), f32),
             pltpu.VMEM((STEPS, dom_count, BLOCK // 2, 2 * BLOCK), f32),
             pltpu.VMEM((STEPS, BLOCK, width), f32),
+            pltpu.VMEM((STEPS, blk_count, own, STORED), f32),
+            pltpu.VMEM((PIECES, each, STORED), f32),
+            pltpu.VMEM((dom_count, each, STORED), f32),
+            pltpu.VMEM((blk_count, PIECES, each, STORED), f32),
+            pltpu.VMEM((STORED, STORED), f32),
+            pltpu.VMEM((STORED, STORED), bf16),
+            pltpu.VMEM((STORED, STORED), bf16),
             dma((tiles,)),
             dma((blk_count,)), dma,
             dma((3,)), dma((3,)),
@@ -312,6 +429,10 @@
             dma((sums, dom_count)), dma((sums, dom_count)),
             dma((STEPS, blk_count)), dma((STEPS, blk_count)),
             dma((STEPS, dom_count)), dma((STEPS, dom_count)),
+            dma((STEPS, blk_count)), dma((STEPS, blk_count)),
+            dma((dom_count,)), dma((dom_count,)),
+            dma((dom_count,)), dma((dom_count,)),
+            dma((blk_count,)), dma((blk_count,)),
         ],
         compiler_params=pltpu.CompilerParams(
             collective_id=0, has_side_effects=True, vmem_limit_bytes=56 * 1024 * 1024

time: 102 us -> 92.4 us (0.906)
  Pallas kernels: 96.6 us -> 87.1 us
    pallas_call x1, Pallas kernels: 96.6 us -> 87.1 us  [local(): pl.pallas_call(functools.partial(kernel, dom_count, blk_count), out_shape...]
where the time goes in v3:
time: 92.4 us; the launch traced here: 92.1 us
  Pallas kernels  87.1 us (94%)
  local copies, waits for them, and re-layouts  3.61 us (4%)
    pallas_call x1, Pallas kernels, local(): pl.pallas_call(functools.partial(kernel, dom_count, blk_count), out_shape...  87.1 us
    unnamed x2, local copies, waits for them, and re-layouts  3.01 us

profile of v3, /device:TPU:0, one launch (start us, length us, event | category | flops | bytes accessed | tf_op | source)
XLA Modules:
  0.0 92.1 jit_solution(4907112034860664882)
XLA Ops:
  0.6 0.8 fusion.5
  1.4 0.6 reshape.8.slots_ref
  2.0 87.1 %lanczos.1 = (f32[2,16,768]{2,1,0:T(8,128)}, f32[2,64,64]{2,1,0:T(8,128)}) custom-call(s32[60]{0:T(128)} %reshape.8.slots_ref, f32[4,15,192,192]{3,2,1,0:T(8,128)} %hess_ref.1, f32[128,768]{1,0:T(8,128)} %basis_ref.1), custom_call_target="tpu_custom_call" | custom-call | tf_op jit(solution)/shard_map/lanczos/pallas_call | solution.py:392
  89.1 1.5 %copy.8 = f32[2,16,768]{2,1,0:T(8,128)} copy(f32[2,16,768]{2,1,0:T(8,128)} %get-tuple-element.4) | data formatting | bytes 196608
  90.7 1.5 %copy.9 = f32[2,64,64]{2,1,0:T(8,128)} copy(f32[2,64,64]{2,1,0:T(8,128)} %get-tuple-element.5) | data formatting | bytes 65536

commit v4 on v3

--- a/solution.py
+++ b/solution.py
@@ -274,7 +274,7 @@
         total = total / row_total
         return jnp.concatenate([total[:, :BLOCK], total[:, BLOCK:]], axis=0)
 
-    def summed(a, value, meanwhile):
+    def summed(a, value, meanwhile, later=None):
         lanes = STORED // LANE
         for j in range(PIECES):
             h, q = divmod(j, lanes)
@@ -296,6 +296,8 @@
         when(owner, reduce)
         for o in range(1, dom_count):
             send(owner, coef.at[a, mine], coef.at[a, mine], ag_s.at[a, o], ag_r.at[a, o], (dom_peer(o), me_b))
+        if later is not None:
+            later()
         for o in range(1, dom_count):
             origin = dom_peer(-o)
             cond = None if all_own else origin < PIECES
@@ -347,7 +349,8 @@
             send_pending(step, pending)
             both = stacked(pending)
             inner = folded((dot(stored_hi[...], both, NT) + dot(stored_lo[...], both, NT)).T)
-            send_coef(step, summed(SWEEPS, inner, functools.partial(send_gram, step)))
+            send_gram_later = functools.partial(send_gram, step)
+            send_coef(step, summed(SWEEPS, inner, send_gram_later, functools.partial(replace_mat, inverse)))
             first = all_coef(step)
             second = first - times_mat(first)
             left = second - times_mat(second)
@@ -369,7 +372,6 @@
             high, low = halves(new)
             stored_hi[:BLOCK] = high
             stored_lo[:BLOCK] = low
-            replace_mat(inverse)
 
     for cond, copy in sent:
         when(cond, copy.wait_send)

time: 92.4 us -> 92.1 us (level)
  no operation moved by 1% of the time
where the time goes in v4:
time: 92.1 us; the launch traced here: 91.8 us
  Pallas kernels  86.8 us (94%)
  local copies, waits for them, and re-layouts  3.61 us (4%)
    pallas_call x1, Pallas kernels, local(): pl.pallas_call(functools.partial(kernel, dom_count, blk_count), out_shape...  86.8 us
    unnamed x2, local copies, waits for them, and re-layouts  3.01 us

profile of v4, /device:TPU:0, one launch (start us, length us, event | category | flops | bytes accessed | tf_op | source)
XLA Modules:
  0.0 91.8 jit_solution(645075549208242504)
XLA Ops:
  0.6 0.8 fusion.5
  1.4 0.6 reshape.8.slots_ref
  2.0 86.8 %lanczos.1 = (f32[2,16,768]{2,1,0:T(8,128)}, f32[2,64,64]{2,1,0:T(8,128)}) custom-call(s32[60]{0:T(128)} %reshape.8.slots_ref, f32[4,15,192,192]{3,2,1,0:T(8,128)} %hess_ref.1, f32[128,768]{1,0:T(8,128)} %basis_ref.1), custom_call_target="tpu_custom_call" | custom-call | tf_op jit(solution)/shard_map/lanczos/pallas_call | solution.py:394
  88.8 1.5 %copy.8 = f32[2,16,768]{2,1,0:T(8,128)} copy(f32[2,16,768]{2,1,0:T(8,128)} %get-tuple-element.4) | data formatting | bytes 196608
  90.4 1.5 %copy.9 = f32[2,64,64]{2,1,0:T(8,128)} copy(f32[2,64,64]{2,1,0:T(8,128)} %get-tuple-element.5) | data formatting | bytes 65536
